TPU v7x, 32 devices: a whole 2x2x4 slice. The times are simulated.
32 devices in a mesh: xy: 8 (over y, x, core), gz: 4 (over z).
Axes of the slice: x: 2, y: 2, z: 4, core: 2. Of those that a mesh axis runs over, the one named last changes fastest.
Arguments:
- density: float32 [1024, 2048], P('xy', 'gz'), may hold values from 0 to 1
- cotangent: float32 [6, 16, 128, 256], P(None, 'gz', 'xy'), may hold values from -6 to 6
- slope: int32 [16], P('gz'), may hold values from 0 to 4
- layer_block: int32 [16], P('gz'), may hold values from 0 to 3
- block_eps: float32 [4, 2], replicated, may hold values from 1.5 to 12
Outputs:
- grad_filtered: float32 [1024, 2048], P('xy', 'gz')
- grad_density: float32 [1024, 2048], P('xy', 'gz')
All inputs are finite; a program needn't handle non-finite values.
Results may differ from a plain program's by a relative error of at most 0.0003.
Values sent between devices are 32-bit elements; how exact they have to be, the bound alone decides.
A program may use at most 64 MiB of HBM per device.

v0:
```python
import jax
import jax.numpy as jnp
from jax import lax
from jax.sharding import PartitionSpec as P

SUB = 8
RADIUS = 32
MATS = 4


def padded_2(value, sides, width):
    for axis, dim in sides:
        count, length = (lax.axis_size(axis), value.shape[dim])
        up = [(i, (i + 1) % count) for i in range(count - 1)]
        down = [(j, i) for i, j in up]
        last = lax.slice_in_dim(value, length - width, length, axis=dim)
        leading = lax.slice_in_dim(value, 0, width, axis=dim)
        before = lax.ppermute(last, axis, up)
        after = lax.ppermute(leading, axis, down)
        value = jnp.concatenate([before, value, after], axis=dim)
    return value


def band(width):
    rows = lax.broadcasted_iota(jnp.int32, (width + 2 * RADIUS, width), 0)
    cols = lax.broadcasted_iota(jnp.int32, (width + 2 * RADIUS, width), 1)
    offset = rows - cols
    values = (RADIUS + 1 - jnp.abs(offset - RADIUS)).astype(jnp.float32) / float((RADIUS + 1) ** 2)
    return jnp.where((offset >= 0) & (offset <= 2 * RADIUS), values, 0.0)


def smooth(padded):
    height = padded.shape[0] - 2 * RADIUS
    width = padded.shape[1] - 2 * RADIUS
    step_cols = 256
    matrix = band(step_cols)
    pieces = []
    for index in range(width // step_cols):
        part = padded[:, index * step_cols : index * step_cols + step_cols + 2 * RADIUS]
        pieces.append(jnp.dot(part, matrix, precision=lax.Precision.HIGHEST))
    across = jnp.concatenate(pieces, axis=1)
    return jnp.dot(band(height).T, across, precision=lax.Precision.HIGHEST)


def row_pooling(height):
    cells = height // SUB
    rows = lax.broadcasted_iota(jnp.int32, (2 * cells, height), 0)
    pixel = lax.broadcasted_iota(jnp.int32, (2 * cells, height), 1)
    cell_row = jnp.where(rows < cells, rows, rows - cells)
    inside = pixel // SUB == cell_row
    place = (2.0 * (pixel % SUB).astype(jnp.float32) + 1.0 - SUB) / 2.0
    values = jnp.where(rows < cells, 1.0, place) / float(SUB)
    return jnp.where(inside, values, 0.0)


def col_pooling(width):
    cells = width // SUB
    pixel = lax.broadcasted_iota(jnp.int32, (width, cells), 0)
    cols = lax.broadcasted_iota(jnp.int32, (width, cells), 1)
    inside = pixel // SUB == cols
    place = (2.0 * (pixel % SUB).astype(jnp.float32) + 1.0 - SUB) / 2.0
    mean_cols = jnp.where(inside, 1.0 / float(SUB), 0.0)
    offset_cols = jnp.where(inside, place / float(SUB), 0.0)
    return (mean_cols, offset_cols)


def cell_tensor(field, params):
    eta, lift, eps_one, eps_two = (params[0], params[1], params[2], params[3])
    height, width = field.shape
    cells = height // SUB
    fill = jax.nn.sigmoid(32.0 * (field - eta))
    pooled_rows = jnp.dot(row_pooling(height), fill, precision=lax.Precision.HIGHEST)
    mean_cols, offset_cols = col_pooling(width)
    both = jnp.dot(pooled_rows, mean_cols, precision=lax.Precision.HIGHEST)
    frac = both[:cells]
    grad_x = both[cells:]
    grad_y = jnp.dot(pooled_rows[:cells], offset_cols, precision=lax.Precision.HIGHEST)
    normsq = grad_x * grad_x + grad_y * grad_y + lift * lift
    mean_eps = eps_two + frac * (eps_one - eps_two)
    mean_inv = 1.0 / eps_two + frac * (1.0 / eps_one - 1.0 / eps_two)
    weight = (1.0 / mean_inv - mean_eps) / normsq
    return jnp.stack(
        [
            mean_eps + weight * grad_x * grad_x,
            mean_eps + weight * grad_y * grad_y,
            mean_eps + weight * lift * lift,
            weight * grad_x * grad_y,
            weight * grad_x * lift,
            weight * grad_y * lift,
        ]
    )


def pull_layers(field, cotangent, table):

    def step(index, total):
        params = lax.dynamic_index_in_dim(table, index, 1, keepdims=False)
        weights = lax.dynamic_index_in_dim(cotangent, index, 1, keepdims=False)
        pullback = jax.vjp(lambda inner: cell_tensor(inner, params), field)[1]
        return total + pullback(weights)[0]

    return lax.fori_loop(0, cotangent.shape[1], step, jnp.zeros_like(field))


def backward_piece(own):
    padded = padded_2(own, (("xy", 0), ("gz", 1)), RADIUS)
    return smooth(padded)


def on_device(density, cotangent, slope, layer_block, block_eps):
    level = slope.astype(jnp.float32)
    onehot = (layer_block[:, None] == jnp.arange(MATS)[None, :]).astype(jnp.float32)
    pairs = jnp.dot(onehot, block_eps, precision=lax.Precision.HIGHEST)
    table = jnp.stack([0.5 + 0.02 * (level - 2.0), 0.2 * (1.0 + level), pairs[:, 0], pairs[:, 1]])
    strip = lax.all_gather(density, "gz", axis=1, tiled=True)
    padded = padded_2(strip, (("xy", 0),), RADIUS)
    padded = jnp.pad(padded, ((0, 0), (RADIUS, RADIUS)))
    filtered = smooth(padded)
    partial_grad = pull_layers(filtered, cotangent, table)
    own = lax.psum_scatter(partial_grad, "gz", scatter_dimension=1, tiled=True)
    result = backward_piece(own)
    return (own, result)


def solution(mesh):
    return jax.shard_map(
        on_device,
        mesh=mesh,
        in_specs=(P("xy", "gz"), P(None, "gz", "xy", None), P("gz"), P("gz"), P()),
        out_specs=(P("xy", "gz"), P("xy", "gz")),
        check_vma=False,
    )
```

profile of v0, /device:TPU:1, one launch (start us, length us, event | category | flops | bytes accessed | tf_op | source)
XLA Modules:
  0.0 195.6 jit_solution(1287768417668712064)
XLA Ops:
  7.2 0.7 all-gather.2.cloned.1.call-update
  8.0 0.8 fusion.205
  8.8 30.7 %all-gather.2.cloned.1.call-done = f32[128,2048]{1,0:T(8,128)} async-done(((f32[128,512]{1,0:T(8,128)}), f32[128,2048]{1,0:T(8,128)}) %all-gather.2.cloned.1.call-update) | async-done | bytes 1048592 | tf_op jit(solution)/shard_map/all_gather | solution.py:115
  39.5 1.2 fusion.283
  40.7 3.8 %collective-permute-start = (f32[32,2048]{1,0:T(8,128)S(1)}, f32[32,2048]{1,0:T(8,128)S(1)}, u32[]{:S(2)}, u32[]{:S(2)}) collective-permute-start(f32[32,2048]{1,0:T(8,128)S(1)} %get-tuple-element.262), channel_id=1, source_target_pairs={{0,4},{4,8},{8,12},{12,16},{16,20},{20,24},{24,28},{1,5},{5,9},{9,... | collective-permute-start | bytes 786440 | tf_op jit(solution)/shard_map/ppermute | solution.py:18
  44.5 0.7 add_bitcast_fusion
  45.1 1.9 collective-permute-start.1
  47.1 0.7 collective-permute-done
  47.8 0.1 constant_dynamic-update-slice_fusion.1
  47.9 4.9 %collective-permute-done.1 = f32[32,2048]{1,0:T(8,128)S(1)} collective-permute-done((f32[32,2048]{1,0:T(8,128)S(1)}, f32[32,2048]{1,0:T(8,128)S(1)}, u32[]{:S(2)}, u32[]{:S(2)}) %collective-permute-start.1) | collective-permute-done | bytes 262176 | tf_op jit(solution)/shard_map/ppermute | solution.py:19
  52.8 0.5 convolution_dynamic-update-slice_fusion.7
  53.4 0.5 convolution_dynamic-update-slice_fusion.6
  53.9 0.5 convolution_dynamic-update-slice_fusion.5
  54.5 0.5 convolution_dynamic-update-slice_fusion.4
  55.0 0.5 convolution_dynamic-update-slice_fusion.3
  55.6 0.5 convolution_dynamic-update-slice_fusion.2
  56.1 0.5 convolution_dynamic-update-slice_fusion.1
  56.7 0.5 convolution_dynamic-update-slice_fusion
  57.3 1.1 fusion.193
  58.4 84.3 %while.19 = (s32[]{:T(128)}, f32[128,2048]{1,0:T(8,128)S(1)}, f32[4,4]{1,0:T(4,128)S(1)}, f32[128,2048]{1,0:T(8,128)S(1)}, f32[6,4,16,256]{3,2,1,0:T(8,128)S(1)}...) while((s32[]{:T(128)}, f32[128,2048]{1,0:T(8,128)S(1)}, ...), condition=%wide.region_1.2_spmd.clone, body=%wide.region_0.1_spmd.clone.sunk | while | flops 821595840 | bytes 6284947 | solution.py:102
  58.6 0.1 constant_dynamic-slice_fusion.2
  58.7 0.6 fusion.308
  59.3 1.5 fusion.309
  60.9 1.7 fusion.310
  66.6 3.7 %add_add_fusion.8 = (f32[16,256]{1,0:T(8,128)S(1)}, f32[16,256]{1,0:T(8,128)S(1)}, f32[16,256]{1,0:T(8,128)S(1)}) fusion(f32[6,4,16,256]{3,2,1,0:T(8,128)S(1)} %get-tuple-element.370, s32[]{:T(128)S(6)} %add.444, s32[]{:T(128)} %get-tuple-element.353, s32[]{:T(128)S(6)} %add.445, f32[32,256]{1,0:T(8,128)S(1)} %fusion.310, f32[]{:T(128)} %bitcast.96, ...), kind=kOutput, calls=%fused_computation.49.clone.1 | convolution fusion | flops 105033728 | bytes 350244 | tf_op jit(solution)/shard_map/while/body/eval_jaxpr/jvp()/dot_general | solution.py:77
  70.4 4.5 %fusion.311 = f32[16,2048]{1,0:T(8,128)S(1)} fusion(s32[2048]{0:T(1024)S(1)} %get-tuple-element.324, s32[2048]{0:T(1024)S(1)} %get-tuple-element.325, s32[2048]{0:T(1024)S(1)} %get-tuple-element.321, s32[2048]{0:T(1024)S(1)} %get-tuple-element.322, pred[2048]{0:T(1024)(128)(4,1)S(1)} %get-tuple-element.326, ...), kind=kOutput, calls=%fused_computation.9.clone.1 | convolution fusion | flops 104980480 | bytes 282664 | tf_op jit(solution)/shard_map/while/body/eval_jaxpr/transpose(jvp())/dot_general | solution.py:77
  74.9 2.4 %fusion.312 = f32[32,2048]{1,0:T(8,128)S(1)} fusion(s32[2048]{0:T(1024)S(1)} %get-tuple-element.321, s32[2048]{0:T(1024)S(1)} %get-tuple-element.322, pred[2048]{0:T(1024)(128)(4,1)S(1)} %get-tuple-element.323, f32[16,2048]{1,0:T(8,128)S(1)} %fusion.311, f32[16,256]{1,0:T(8,128)S(1)} %multiply_add_fusion.6, f32[16,256]{1,0:T(8,128)S(1)} %get-tuple-element.339), kind=kOutput, calls=%fused_computation.7.clone.1 | convolution fusion | flops 202973184 | bytes 444416 | tf_op jit(solution)/shard_map/while/body/eval_jaxpr/transpose(jvp())/dot_general | solution.py:74
  77.3 2.3 %fusion.313 = f32[128,2048]{1,0:T(8,128)S(1)} fusion(f32[32,2048]{1,0:T(8,128)S(1)} %fusion.312, f32[128,2048]{1,0:T(8,128)S(1)} %get-tuple-element.354, pred[]{:T(512)S(6)} %compare.15, f32[128,2048]{1,0:T(8,128)S(1)} %get-tuple-element.369, f32[]{:T(128)} %bitcast.95, s32[128]{0:T(128)S(1)} %get-tuple-element.328, s32[128]{0:T(128)S(1)} %get-tuple-element.329, ...), kind=kOutput, calls=%fused_computation.6.clone.1 | convolution fusion | flops 103591936 | bytes 3410341 | tf_op jit(solution)/shard_map/while/body/eval_jaxpr/transpose(jvp())/dot_general | solution.py:72
  79.7 0.6 fusion.308
  80.3 1.5 fusion.309
  81.9 1.7 fusion.310
  87.7 3.7 %add_add_fusion.8 = (f32[16,256]{1,0:T(8,128)S(1)}, f32[16,256]{1,0:T(8,128)S(1)}, f32[16,256]{1,0:T(8,128)S(1)}) fusion(f32[6,4,16,256]{3,2,1,0:T(8,128)S(1)} %get-tuple-element.370, s32[]{:T(128)S(6)} %add.444, s32[]{:T(128)} %get-tuple-element.353, s32[]{:T(128)S(6)} %add.445, f32[32,256]{1,0:T(8,128)S(1)} %fusion.310, f32[]{:T(128)} %bitcast.96, ...), kind=kOutput, calls=%fused_computation.49.clone.1 | convolution fusion | flops 105033728 | bytes 350244 | tf_op jit(solution)/shard_map/while/body/eval_jaxpr/jvp()/dot_general | solution.py:77
  91.4 4.5 %fusion.311 = f32[16,2048]{1,0:T(8,128)S(1)} fusion(s32[2048]{0:T(1024)S(1)} %get-tuple-element.324, s32[2048]{0:T(1024)S(1)} %get-tuple-element.325, s32[2048]{0:T(1024)S(1)} %get-tuple-element.321, s32[2048]{0:T(1024)S(1)} %get-tuple-element.322, pred[2048]{0:T(1024)(128)(4,1)S(1)} %get-tuple-element.326, ...), kind=kOutput, calls=%fused_computation.9.clone.1 | convolution fusion | flops 104980480 | bytes 282664 | tf_op jit(solution)/shard_map/while/body/eval_jaxpr/transpose(jvp())/dot_general | solution.py:77
  95.9 2.4 %fusion.312 = f32[32,2048]{1,0:T(8,128)S(1)} fusion(s32[2048]{0:T(1024)S(1)} %get-tuple-element.321, s32[2048]{0:T(1024)S(1)} %get-tuple-element.322, pred[2048]{0:T(1024)(128)(4,1)S(1)} %get-tuple-element.323, f32[16,2048]{1,0:T(8,128)S(1)} %fusion.311, f32[16,256]{1,0:T(8,128)S(1)} %multiply_add_fusion.6, f32[16,256]{1,0:T(8,128)S(1)} %get-tuple-element.339), kind=kOutput, calls=%fused_computation.7.clone.1 | convolution fusion | flops 202973184 | bytes 444416 | tf_op jit(solution)/shard_map/while/body/eval_jaxpr/transpose(jvp())/dot_general | solution.py:74
  98.3 2.3 %fusion.313 = f32[128,2048]{1,0:T(8,128)S(1)} fusion(f32[32,2048]{1,0:T(8,128)S(1)} %fusion.312, f32[128,2048]{1,0:T(8,128)S(1)} %get-tuple-element.354, pred[]{:T(512)S(6)} %compare.15, f32[128,2048]{1,0:T(8,128)S(1)} %get-tuple-element.369, f32[]{:T(128)} %bitcast.95, s32[128]{0:T(128)S(1)} %get-tuple-element.328, s32[128]{0:T(128)S(1)} %get-tuple-element.329, ...), kind=kOutput, calls=%fused_computation.6.clone.1 | convolution fusion | flops 103591936 | bytes 3410341 | tf_op jit(solution)/shard_map/while/body/eval_jaxpr/transpose(jvp())/dot_general | solution.py:72
  100.7 0.6 fusion.308
  101.4 1.5 fusion.309
  102.9 1.7 fusion.310
  108.7 3.7 %add_add_fusion.8 = (f32[16,256]{1,0:T(8,128)S(1)}, f32[16,256]{1,0:T(8,128)S(1)}, f32[16,256]{1,0:T(8,128)S(1)}) fusion(f32[6,4,16,256]{3,2,1,0:T(8,128)S(1)} %get-tuple-element.370, s32[]{:T(128)S(6)} %add.444, s32[]{:T(128)} %get-tuple-element.353, s32[]{:T(128)S(6)} %add.445, f32[32,256]{1,0:T(8,128)S(1)} %fusion.310, f32[]{:T(128)} %bitcast.96, ...), kind=kOutput, calls=%fused_computation.49.clone.1 | convolution fusion | flops 105033728 | bytes 350244 | tf_op jit(solution)/shard_map/while/body/eval_jaxpr/jvp()/dot_general | solution.py:77
  112.4 4.5 %fusion.311 = f32[16,2048]{1,0:T(8,128)S(1)} fusion(s32[2048]{0:T(1024)S(1)} %get-tuple-element.324, s32[2048]{0:T(1024)S(1)} %get-tuple-element.325, s32[2048]{0:T(1024)S(1)} %get-tuple-element.321, s32[2048]{0:T(1024)S(1)} %get-tuple-element.322, pred[2048]{0:T(1024)(128)(4,1)S(1)} %get-tuple-element.326, ...), kind=kOutput, calls=%fused_computation.9.clone.1 | convolution fusion | flops 104980480 | bytes 282664 | tf_op jit(solution)/shard_map/while/body/eval_jaxpr/transpose(jvp())/dot_general | solution.py:77
  116.9 2.4 %fusion.312 = f32[32,2048]{1,0:T(8,128)S(1)} fusion(s32[2048]{0:T(1024)S(1)} %get-tuple-element.321, s32[2048]{0:T(1024)S(1)} %get-tuple-element.322, pred[2048]{0:T(1024)(128)(4,1)S(1)} %get-tuple-element.323, f32[16,2048]{1,0:T(8,128)S(1)} %fusion.311, f32[16,256]{1,0:T(8,128)S(1)} %multiply_add_fusion.6, f32[16,256]{1,0:T(8,128)S(1)} %get-tuple-element.339), kind=kOutput, calls=%fused_computation.7.clone.1 | convolution fusion | flops 202973184 | bytes 444416 | tf_op jit(solution)/shard_map/while/body/eval_jaxpr/transpose(jvp())/dot_general | solution.py:74
  119.3 2.3 %fusion.313 = f32[128,2048]{1,0:T(8,128)S(1)} fusion(f32[32,2048]{1,0:T(8,128)S(1)} %fusion.312, f32[128,2048]{1,0:T(8,128)S(1)} %get-tuple-element.354, pred[]{:T(512)S(6)} %compare.15, f32[128,2048]{1,0:T(8,128)S(1)} %get-tuple-element.369, f32[]{:T(128)} %bitcast.95, s32[128]{0:T(128)S(1)} %get-tuple-element.328, s32[128]{0:T(128)S(1)} %get-tuple-element.329, ...), kind=kOutput, calls=%fused_computation.6.clone.1 | convolution fusion | flops 103591936 | bytes 3410341 | tf_op jit(solution)/shard_map/while/body/eval_jaxpr/transpose(jvp())/dot_general | solution.py:72
  121.7 0.6 fusion.308
  122.4 1.5 fusion.309
  123.9 1.7 fusion.310
  129.7 3.7 %add_add_fusion.8 = (f32[16,256]{1,0:T(8,128)S(1)}, f32[16,256]{1,0:T(8,128)S(1)}, f32[16,256]{1,0:T(8,128)S(1)}) fusion(f32[6,4,16,256]{3,2,1,0:T(8,128)S(1)} %get-tuple-element.370, s32[]{:T(128)S(6)} %add.444, s32[]{:T(128)} %get-tuple-element.353, s32[]{:T(128)S(6)} %add.445, f32[32,256]{1,0:T(8,128)S(1)} %fusion.310, f32[]{:T(128)} %bitcast.96, ...), kind=kOutput, calls=%fused_computation.49.clone.1 | convolution fusion | flops 105033728 | bytes 350244 | tf_op jit(solution)/shard_map/while/body/eval_jaxpr/jvp()/dot_general | solution.py:77
  133.4 4.5 %fusion.311 = f32[16,2048]{1,0:T(8,128)S(1)} fusion(s32[2048]{0:T(1024)S(1)} %get-tuple-element.324, s32[2048]{0:T(1024)S(1)} %get-tuple-element.325, s32[2048]{0:T(1024)S(1)} %get-tuple-element.321, s32[2048]{0:T(1024)S(1)} %get-tuple-element.322, pred[2048]{0:T(1024)(128)(4,1)S(1)} %get-tuple-element.326, ...), kind=kOutput, calls=%fused_computation.9.clone.1 | convolution fusion | flops 104980480 | bytes 282664 | tf_op jit(solution)/shard_map/while/body/eval_jaxpr/transpose(jvp())/dot_general | solution.py:77
  137.9 2.4 %fusion.312 = f32[32,2048]{1,0:T(8,128)S(1)} fusion(s32[2048]{0:T(1024)S(1)} %get-tuple-element.321, s32[2048]{0:T(1024)S(1)} %get-tuple-element.322, pred[2048]{0:T(1024)(128)(4,1)S(1)} %get-tuple-element.323, f32[16,2048]{1,0:T(8,128)S(1)} %fusion.311, f32[16,256]{1,0:T(8,128)S(1)} %multiply_add_fusion.6, f32[16,256]{1,0:T(8,128)S(1)} %get-tuple-element.339), kind=kOutput, calls=%fused_computation.7.clone.1 | convolution fusion | flops 202973184 | bytes 444416 | tf_op jit(solution)/shard_map/while/body/eval_jaxpr/transpose(jvp())/dot_general | solution.py:74
  140.4 2.3 %fusion.313 = f32[128,2048]{1,0:T(8,128)S(1)} fusion(f32[32,2048]{1,0:T(8,128)S(1)} %fusion.312, f32[128,2048]{1,0:T(8,128)S(1)} %get-tuple-element.354, pred[]{:T(512)S(6)} %compare.15, f32[128,2048]{1,0:T(8,128)S(1)} %get-tuple-element.369, f32[]{:T(128)} %bitcast.95, s32[128]{0:T(128)S(1)} %get-tuple-element.328, s32[128]{0:T(128)S(1)} %get-tuple-element.329, ...), kind=kOutput, calls=%fused_computation.6.clone.1 | convolution fusion | flops 103591936 | bytes 3410341 | tf_op jit(solution)/shard_map/while/body/eval_jaxpr/transpose(jvp())/dot_general | solution.py:72
  142.7 1.0 copy-done.2
  143.7 26.1 %reduce-scatter.2.cloned.1.call-done = f32[128,512]{1,0:T(8,128)} async-done(((f32[128,2048]{1,0:T(8,128)}), f32[128,512]{1,0:T(8,128)}) %reduce-scatter.2.cloned.1.call-update) | async-done | bytes 262160 | tf_op jit(solution)/shard_map/reduce_scatter | solution.py:120
  169.8 0.9 fusion.285
  170.7 3.8 %collective-permute-start.2 = (f32[32,512]{1,0:T(8,128)S(1)}, f32[32,512]{1,0:T(8,128)S(1)}, u32[]{:S(2)}, u32[]{:S(2)}) collective-permute-start(f32[32,512]{1,0:T(8,128)S(1)} %get-tuple-element.266), channel_id=1, source_target_pairs={{0,4},{4,8},{8,12},{12,16},{16,20},{20,24},{24,28},{1,5},{5,9},{9,... | collective-permute-start | bytes 196616 | tf_op jit(solution)/shard_map/ppermute | solution.py:18
  174.5 1.9 collective-permute-start.3
  176.5 1.0 constant_dynamic-update-slice_fusion.4
  177.4 2.7 %collective-permute-done.3 = f32[32,512]{1,0:T(8,128)S(1)} collective-permute-done((f32[32,512]{1,0:T(8,128)S(1)}, f32[32,512]{1,0:T(8,128)S(1)}, u32[]{:S(2)}, u32[]{:S(2)}) %collective-permute-start.3) | collective-permute-done | bytes 65568 | tf_op jit(solution)/shard_map/ppermute | solution.py:19
  180.1 0.1 fusion.284
  180.2 1.3 collective-permute-start.4
  181.5 1.3 collective-permute-start.5
  182.8 0.3 collective-permute-done.4
  183.1 0.5 fusion.131
  183.7 3.4 %collective-permute-done.5 = f32[192,32]{1,0:T(8,128)S(1)} collective-permute-done((f32[192,32]{1,0:T(8,128)S(1)}, f32[192,32]{1,0:T(8,128)S(1)}, u32[]{:S(2)}, u32[]{:S(2)}) %collective-permute-start.5) | collective-permute-done | bytes 24608 | tf_op jit(solution)/shard_map/ppermute | solution.py:19
  187.1 0.6 fusion.130
  187.6 1.1 fusion.124
  (57 shorter events, 0.7 us)
Async XLA Ops:
  7.2 0.8 copy-start
  7.2 32.3 %all-gather.2.cloned.1.call-start = ((), (), s32[]{:S(2)}) async-start(), calls=%async_computation.1 | async-start | bytes 1310720 | tf_op jit(solution)/shard_map/all_gather | solution.py:115
  7.9 161.9 %reduce-scatter.2.cloned.1.call-start = ((), (), s32[]{:S(2)}) async-start(), calls=%async_computation.2 | async-start | bytes 1310720 | tf_op jit(solution)/shard_map/reduce_scatter | solution.py:120
  39.5 8.3 %copy-start.1 = (f32[128,2048]{1,0:T(8,128)S(1)}, f32[128,2048]{1,0:T(8,128)}, u32[]{:S(2)}) copy-start(f32[128,2048]{1,0:T(8,128)} %all-gather.2.cloned.1.call-done) | copy-start | bytes 3145732
  40.7 7.1 %collective-permute-start = (f32[32,2048]{1,0:T(8,128)S(1)}, f32[32,2048]{1,0:T(8,128)S(1)}, u32[]{:S(2)}, u32[]{:S(2)}) collective-permute-start(f32[32,2048]{1,0:T(8,128)S(1)} %get-tuple-element.262), channel_id=1, source_target_pairs={{0,4},{4,8},{8,12},{12,16},{16,20},{20,24},{24,28},{1,5},{5,9},{9,... | collective-permute-start | bytes 786440 | tf_op jit(solution)/shard_map/ppermute | solution.py:18
  45.1 7.7 %collective-permute-start.1 = (f32[32,2048]{1,0:T(8,128)S(1)}, f32[32,2048]{1,0:T(8,128)S(1)}, u32[]{:S(2)}, u32[]{:S(2)}) collective-permute-start(f32[32,2048]{1,0:T(8,128)S(1)} %get-tuple-element.261), channel_id=1, source_target_pairs={{4,0},{8,4},{12,8},{16,12},{20,16},{24,20},{28,24},{5,1},{9,5},{13... | collective-permute-start | bytes 786440 | tf_op jit(solution)/shard_map/ppermute | solution.py:19
  57.3 1.2 copy-start.3
  142.7 1.0 copy-start.2
  170.7 5.8 %collective-permute-start.2 = (f32[32,512]{1,0:T(8,128)S(1)}, f32[32,512]{1,0:T(8,128)S(1)}, u32[]{:S(2)}, u32[]{:S(2)}) collective-permute-start(f32[32,512]{1,0:T(8,128)S(1)} %get-tuple-element.266), channel_id=1, source_target_pairs={{0,4},{4,8},{8,12},{12,16},{16,20},{20,24},{24,28},{1,5},{5,9},{9,... | collective-permute-start | bytes 196616 | tf_op jit(solution)/shard_map/ppermute | solution.py:18
  174.5 5.6 %collective-permute-start.3 = (f32[32,512]{1,0:T(8,128)S(1)}, f32[32,512]{1,0:T(8,128)S(1)}, u32[]{:S(2)}, u32[]{:S(2)}) collective-permute-start(f32[32,512]{1,0:T(8,128)S(1)} %get-tuple-element.265), channel_id=1, source_target_pairs={{4,0},{8,4},{12,8},{16,12},{20,16},{24,20},{28,24},{5,1},{9,5},{13... | collective-permute-start | bytes 196616 | tf_op jit(solution)/shard_map/ppermute | solution.py:19
  180.2 2.9 %collective-permute-start.4 = (f32[192,32]{1,0:T(8,128)S(1)}, f32[192,32]{1,0:T(8,128)S(1)}, u32[]{:S(2)}, u32[]{:S(2)}) collective-permute-start(f32[192,32]{1,0:T(8,128)S(1)} %get-tuple-element.263), channel_id=1, source_target_pairs={{0,1},{1,2},{2,3},{4,5},{5,6},{6,7},{8,9},{9,10},{10,11},{12,13},{... | collective-permute-start | bytes 73736 | tf_op jit(solution)/shard_map/ppermute | solution.py:18
  181.5 5.6 %collective-permute-start.5 = (f32[192,32]{1,0:T(8,128)S(1)}, f32[192,32]{1,0:T(8,128)S(1)}, u32[]{:S(2)}, u32[]{:S(2)}) collective-permute-start(f32[192,32]{1,0:T(8,128)S(1)} %get-tuple-element.264), channel_id=1, source_target_pairs={{1,0},{2,1},{3,2},{5,4},{6,5},{7,6},{9,8},{10,9},{11,10},{13,12},{... | collective-permute-start | bytes 73736 | tf_op jit(solution)/shard_map/ppermute | solution.py:19
Sparse Core Ops, SparseCore 0:
  9.6 29.8 all-gather.1
  143.8 25.9 reduce-scatter.1
where the time goes:
time: 197 us; the launch traced here: 196 us
  matrix products  72.8 us (37%)
  waiting for transfers between devices  69.5 us (35%)
  loops' own time  17 us (9%)
  between operations  14.3 us (7%)
  starting transfers between devices  14.1 us (7%)
  local copies, waits for them, and re-layouts  6.98 us (4%)
    dot_general x8, matrix products, cell_tensor(): jnp.dot(pooled_rows[:cells], offset_cols, precision=lax.Precision.HIGHEST)  32.6 us
    all_gather x1, waiting for transfers between devices, on_device(): strip = lax.all_gather(density, 'gz', axis=1, tiled=True)  30.7 us
    reduce_scatter x1, waiting for transfers between devices, on_device(): own = lax.psum_scatter(partial_grad, 'gz', scatter_dimension=1, tiled=True)  26.1 us
    another operation x1, loops' own time, pull_layers(): return lax.fori_loop(0, cotangent.shape[1], step, jnp.zeros_like(field))  17 us
    dot_general x8, matrix products, cell_tensor(): both = jnp.dot(pooled_rows, mean_cols, precision=lax.Precision.HIGHEST)  16.5 us
    dot_general x8, matrix products, cell_tensor(): jnp.dot(row_pooling(height), fill, precision=lax.Precision.HIGHEST)  15.2 us
    ppermute x3, waiting for transfers between devices, padded_2(): after = lax.ppermute(leading, axis, down)  11 us
    ppermute x3, starting transfers between devices, padded_2(): before = lax.ppermute(last, axis, up)  8.91 us
  transfers between devices with their start and end apart: 8, of which 7 were waited for; matrix products, arithmetic and copies ran while one was open for 2% of the time, Pallas kernels for 0%

commit v1 on v0

v1 whole, which is shorter than its diff:
```python
import functools

import jax
import jax.numpy as jnp
from jax import lax
from jax.experimental import pallas as pl
from jax.experimental.pallas import tpu as pltpu
from jax.sharding import PartitionSpec as P

SUB = 8
RADIUS = 32
LANES = 128
BAND_COLS = 256
STEEP = 32.0
MESH = pl.DeviceIdType.MESH
F32 = jnp.float32
BF16 = jnp.bfloat16
NEAR = [(dx, dz) for dx in (-1, 0, 1) for dz in (-1, 0, 1) if (dx, dz) != (0, 0)]


def split(value, terms):
    parts = []
    for _ in range(terms):
        part = value.astype(BF16)
        parts.append(part)
        value = value - part.astype(F32)
    return parts


def iota(shape, dim):
    return lax.broadcasted_iota(jnp.int32, shape, dim)


def taps(offset):
    return jnp.maximum(RADIUS + 1 - jnp.abs(offset), 0).astype(F32).astype(BF16)


def col_band():
    shape = (BAND_COLS + 2 * LANES, BAND_COLS)
    return taps(iota(shape, 0) - LANES - iota(shape, 1))


def row_band(height):
    shape = (height, height + 2 * RADIUS)
    return taps(iota(shape, 1) - RADIUS - iota(shape, 0))


def pool_values(cell, place, other):
    offset = (2 * (place % SUB) + 1 - SUB).astype(F32) / 2.0
    inside = place // SUB == cell % other
    values = jnp.where(cell < other, 1.0, offset) / float(SUB)
    return jnp.where(inside, values, 0.0).astype(BF16)


def col_pool(width):
    shape = (width, 2 * width // SUB)
    return pool_values(iota(shape, 1), iota(shape, 0), width // SUB)


def col_pool_t(width):
    shape = (2 * width // SUB, width)
    return pool_values(iota(shape, 0), iota(shape, 1), width // SUB)


def row_pool(height):
    shape = (2 * height // SUB, height)
    return pool_values(iota(shape, 0), iota(shape, 1), height // SUB)


def row_pool_t(height):
    shape = (height, 2 * height // SUB)
    return pool_values(iota(shape, 1), iota(shape, 0), height // SUB)


def dot(a, b):
    return jnp.dot(a, b, preferred_element_type=F32)


def smooth(pad, height, width, terms):
    matrix = col_band()
    rows = row_band(height)
    scale = 1.0 / float((RADIUS + 1) ** 4)
    out = []
    for start in range(0, width, BAND_COLS):
        part = pad[:, start : start + BAND_COLS + 2 * LANES]
        across = sum(dot(x, matrix) for x in split(part, terms))
        total = sum(dot(rows, x) for x in split(across, terms))
        out.append(total * scale)
    return out


def kernel(nx, nz, rows, cols, local, slope, block, eps, density, cot, grad_out, dens_out,
           pad, gpad, stage, recv, par_send, par_recv, filt, soft, hi, lo, pooled,
           halo_send, halo_recv, grad_send, grad_recv, cot_send, cot_recv, pars_send, pars_recv):
    x = lax.axis_index("xy")
    z = lax.axis_index("gz")
    cells_x, cells_y = rows // SUB, cols // SUB
    tall, wide = rows + 2 * RADIUS, cols + 2 * LANES
    mid_r, mid_c = pl.ds(RADIUS, rows), pl.ds(LANES, cols)

    def exists(dx, dz):
        ok = None
        for pos, delta, count in ((x, dx, nx), (z, dz, nz)):
            if delta == -1:
                here = pos > 0
            elif delta == 1:
                here = pos < count - 1
            else:
                continue
            ok = here if ok is None else jnp.logical_and(ok, here)
        return ok

    for ref in (pad, gpad):
        ref[0:RADIUS, :] = jnp.zeros((RADIUS, wide), F32)
        ref[RADIUS + rows : tall, :] = jnp.zeros((RADIUS, wide), F32)
        ref[RADIUS : RADIUS + rows, 0:LANES] = jnp.zeros((rows, LANES), F32)
        ref[RADIUS : RADIUS + rows, LANES + cols : wide] = jnp.zeros((rows, LANES), F32)

    barrier = pltpu.get_barrier_semaphore()
    far = [(dx, dz) for dx, dz in NEAR if dx != 0]
    for k in range(1, nz):
        pl.semaphore_signal(barrier, inc=1, device_id=(x, lax.rem(z + k, nz)), device_id_type=MESH)
    for dx, dz in far:
        @pl.when(exists(dx, dz))
        def _():
            pl.semaphore_signal(barrier, inc=1, device_id=(x + dx, z + dz), device_id_type=MESH)

    half = iota((1, LANES), 1) < cells_y
    level = [slope[l].astype(F32) for l in range(local)]
    lines = [jnp.full((1, LANES), 0.5 + 0.02 * (v - 2.0), F32) for v in level]
    for k in range(local // 2):
        a, b = 2 * k, 2 * k + 1
        lines.append(jnp.where(half, 0.2 * (1.0 + level[a]), 0.2 * (1.0 + level[b])))
        for j in range(2):
            lines.append(jnp.where(half, eps[block[a], j], eps[block[b], j]))
    for i, line in enumerate(lines):
        par_send[i : i + 1, :] = line
    par_send[len(lines) :, :] = jnp.zeros((par_send.shape[0] - len(lines), LANES), F32)

    pl.semaphore_wait(barrier, nz - 1 + sum(jnp.where(exists(dx, dz), 1, 0) for dx, dz in far))

    def halo(source, base_r, base_c, target, send, receive, d):
        dx, dz = NEAR[d]
        src_r = {-1: pl.ds(base_r, RADIUS), 0: pl.ds(base_r, rows), 1: pl.ds(base_r + rows - RADIUS, RADIUS)}[dx]
        dst_r = {-1: pl.ds(RADIUS + rows, RADIUS), 0: mid_r, 1: pl.ds(0, RADIUS)}[dx]
        src_c = {-1: pl.ds(base_c, LANES), 0: pl.ds(base_c, cols), 1: pl.ds(base_c + cols - LANES, LANES)}[dz]
        dst_c = {-1: pl.ds(LANES + cols, LANES), 0: mid_c, 1: pl.ds(0, LANES)}[dz]
        return pltpu.make_async_remote_copy(
            src_ref=source.at[src_r, src_c], dst_ref=target.at[dst_r, dst_c],
            send_sem=send.at[d], recv_sem=receive.at[d],
            device_id=(x + dx, z + dz), device_id_type=MESH)

    def halo_each(args, what):
        for d, (dx, dz) in enumerate(NEAR):
            copy = halo(*args, d)
            where = exists(-dx, -dz) if what == "wait_recv" else exists(dx, dz)
            pl.when(where)(getattr(copy, what))

    first = (density, 0, 0, pad, halo_send, halo_recv)
    second = (gpad, RADIUS, LANES, gpad, grad_send, grad_recv)
    halo_each(first, "start")

    def peer_copy(src, dst, send, receive, k, outgoing):
        peer = lax.rem(z + k, nz)
        slot = z if outgoing else peer
        return pltpu.make_async_remote_copy(
            src_ref=src(peer), dst_ref=dst.at[slot], send_sem=send.at[k], recv_sem=receive.at[slot],
            device_id=(x, peer), device_id_type=MESH)

    def par_copy(k, outgoing):
        return peer_copy(lambda p: par_send, par_recv, pars_send, pars_recv, k, outgoing)

    def cot_copy(k, outgoing):
        return peer_copy(lambda p: stage.at[p], recv, cot_send, cot_recv, k, outgoing)

    for k in range(1, nz):
        par_copy(k, True).start()

    for c in range(cot.shape[0]):
        for k in range(local // 2):
            for h in range(nz // 2):
                a = cot[c, 2 * k, :, h * LANES : (h + 1) * LANES]
                b = cot[c, 2 * k + 1, :, h * LANES : (h + 1) * LANES]
                stage[2 * h, c, k] = jnp.where(half, a, pltpu.roll(b, cells_y, 1))
                stage[2 * h + 1, c, k] = jnp.where(half, pltpu.roll(a, cells_y, 1), b)
    for k in range(1, nz):
        cot_copy(k, True).start()
    par_recv[z] = par_send[...]
    recv[z] = stage[z]

    pad[RADIUS : RADIUS + rows, LANES : LANES + cols] = density[...]
    halo_each(first, "wait_recv")
    for i, part in enumerate(smooth(pad, rows, cols, 3)):
        filt[:, i * BAND_COLS : (i + 1) * BAND_COLS] = part
    for k in range(1, nz):
        par_copy(k, False).wait_recv()

    pool_c = col_pool(cols)
    chunk = 16

    @pl.loop(0, nz)
    def _(g):
        for l in range(local):
            eta = par_recv[g, l : l + 1, :]
            eta = jnp.concatenate([eta] * (cols // LANES), axis=1)

            @pl.loop(0, rows // chunk)
            def _(i):
                at = pl.multiple_of(i * chunk, chunk)
                fill = 1.0 / (1.0 + jnp.exp(STEEP * (eta - filt[pl.ds(at, chunk), :])))
                to = pl.ds(pl.multiple_of(at + l * rows, chunk), chunk)
                soft[g, to, :] = fill * (1.0 - fill)
                upper, lower = split(fill, 2)
                hi[to, :] = upper
                lo[to, :] = lower
        pooled[g] = dot(hi[...], pool_c) + dot(lo[...], pool_c)

    pool_r = row_pool(rows)
    pool_r2 = jnp.concatenate([pool_r, pool_r], axis=1)
    back_r = row_pool_t(rows)
    back_r2 = jnp.concatenate([back_r, back_r], axis=1)
    back_c = col_pool_t(cols)
    for k in range(1, nz):
        cot_copy(k, False).wait_recv()

    gpad[RADIUS : RADIUS + rows, LANES : LANES + cols] = jnp.zeros((rows, cols), F32)

    @pl.loop(0, nz)
    def _(g):
        zs = []
        for k in range(local // 2):
            moments = []
            for l in (2 * k, 2 * k + 1):
                upper, lower = split(pooled[g, l * rows : (l + 1) * rows, :], 2)
                moments.append(dot(pool_r2, jnp.concatenate([upper, lower], axis=0)))
            swap = lambda v: pltpu.roll(v, cells_y, 1)
            top_a, low_a = moments[0][:cells_x], moments[0][cells_x:]
            top_b, low_b = moments[1][:cells_x], moments[1][cells_x:]
            frac = jnp.where(half, top_a, swap(top_b))
            gy = jnp.where(half, swap(top_a), top_b)
            gx = jnp.where(half, low_a, swap(low_b))
            base = local + 3 * k
            cz = par_recv[g, base : base + 1, :]
            e1 = par_recv[g, base + 1 : base + 2, :]
            e2 = par_recv[g, base + 2 : base + 3, :]
            cxx, cyy, czz, cxy, cxz, cyz = (recv[g, c, k] for c in range(6))
            step = e1 - e2
            inv2 = 1.0 / e2
            inv_step = 1.0 / e1 - inv2
            norm = 1.0 / (gx * gx + gy * gy + cz * cz)
            mean = e2 + frac * step
            harm = 1.0 / (inv2 + frac * inv_step)
            weight = (harm - mean) * norm
            px = cxx * gx + cxy * gy + cxz * cz
            py = cyy * gy + cyz * cz
            quad = (gx * px + gy * py + cz * cz * czz) * norm
            d_frac = (cxx + cyy + czz - quad) * step - quad * harm * harm * inv_step
            d_gx = weight * (px + (cxx - 2.0 * quad) * gx)
            d_gy = weight * (py + (cyy - 2.0 * quad) * gy + cxy * gx)
            zero = jnp.zeros_like(d_gx)
            zs += [jnp.where(half, d_frac, swap(d_gy)), jnp.where(half, d_gx, zero),
                   jnp.where(half, swap(d_frac), d_gy), jnp.where(half, swap(d_gx), zero)]
        upper, lower = split(jnp.concatenate(zs, axis=0), 2)
        spread = dot(upper, back_c) + dot(lower, back_c)
        deep = 2 * cells_x
        for l in range(local):
            upper, lower = split(spread[l * deep : (l + 1) * deep], 2)
            pixels = dot(back_r2, jnp.concatenate([upper, lower], axis=0))
            gpad[RADIUS : RADIUS + rows, LANES : LANES + cols] += pixels * soft[g, l * rows : (l + 1) * rows, :]

    own = gpad[RADIUS : RADIUS + rows, LANES : LANES + cols] * STEEP
    gpad[RADIUS : RADIUS + rows, LANES : LANES + cols] = own
    halo_each(second, "start")
    grad_out[...] = own
    halo_each(second, "wait_recv")
    for i, part in enumerate(smooth(gpad, rows, cols, 2)):
        dens_out[:, i * BAND_COLS : (i + 1) * BAND_COLS] = part

    halo_each(first, "wait_send")
    halo_each(second, "wait_send")
    for k in range(1, nz):
        par_copy(k, True).wait_send()
        cot_copy(k, True).wait_send()


def on_device(density, cot, slope, layer_block, block_eps, nx, nz):
    rows, cols = density.shape
    comps, local = cot.shape[:2]
    cells_x = rows // SUB
    tall, wide = rows + 2 * RADIUS, cols + 2 * LANES
    packed = (nz, comps, local // 2, cells_x, LANES)
    vmem = pl.BlockSpec(memory_space=pltpu.VMEM)
    smem = pl.BlockSpec(memory_space=pltpu.SMEM)
    dma = pltpu.SemaphoreType.DMA
    near = len(NEAR)
    shape = jax.ShapeDtypeStruct((rows, cols), F32)
    return pl.pallas_call(
        functools.partial(kernel, nx, nz, rows, cols, local),
        out_shape=(shape, shape),
        in_specs=[smem, smem, smem, vmem, vmem],
        out_specs=(vmem, vmem),
        scratch_shapes=[
            pltpu.VMEM((tall, wide), F32),
            pltpu.VMEM((tall, wide), F32),
            pltpu.VMEM(packed, F32),
            pltpu.VMEM(packed, F32),
            pltpu.VMEM((16, LANES), F32),
            pltpu.VMEM((nz, 16, LANES), F32),
            pltpu.VMEM((rows, cols), F32),
            pltpu.VMEM((nz, local * rows, cols), F32),
            pltpu.VMEM((local * rows, cols), BF16),
            pltpu.VMEM((local * rows, cols), BF16),
            pltpu.VMEM((nz, local * rows, LANES), F32),
            dma((near,)), dma((near,)), dma((near,)), dma((near,)),
            dma((nz,)), dma((nz,)), dma((nz,)), dma((nz,)),
        ],
        compiler_params=pltpu.CompilerParams(
            collective_id=0, has_side_effects=True, vmem_limit_bytes=40 * 1024 * 1024),
    )(slope, layer_block, block_eps, density, cot)


def solution(mesh):
    body = functools.partial(on_device, nx=mesh.shape["xy"], nz=mesh.shape["gz"])
    return jax.shard_map(
        body,
        mesh=mesh,
        in_specs=(P("xy", "gz"), P(None, "gz", "xy", None), P("gz"), P("gz"), P()),
        out_specs=(P("xy", "gz"), P("xy", "gz")),
        check_vma=False,
    )
```

time: 197 us -> 33.3 us (0.17)
  matrix products: 72.8 us -> 0 us
  waiting for transfers between devices: 69.5 us -> 0 us
  Pallas kernels: 0 us -> 28.2 us
  loops' own time: 17 us -> 0 us
  starting transfers between devices: 14.1 us -> 0 us
  between operations: 14.3 us -> 0.66 us
  local copies, waits for them, and re-layouts: 6.98 us -> 4.14 us
    dot_general x37 -> x0, matrix products: 72.8 us -> none  [the longest x8 32.6 us: cell_tensor(): jnp.dot(pooled_rows[:cells], offset_cols, precision=lax.Precision.HIGHEST)]
    all_gather x1 -> x0, waiting for transfers between devices: 30.7 us -> none  [on_device(): strip = lax.all_gather(density, 'gz', axis=1, tiled=True)]
    pallas_call x0 -> x1, Pallas kernels: none -> 28.2 us  [on_device(): pl.pallas_call(functools.partial(kernel, nx, nz, rows, cols, local), out_...]
    reduce_scatter x1 -> x0, waiting for transfers between devices: 26.1 us -> none  [on_device(): own = lax.psum_scatter(partial_grad, 'gz', scatter_dimension=1, tiled=True)]
    another operation x1 -> x0, loops' own time: 17 us -> none  [pull_layers(): return lax.fori_loop(0, cotangent.shape[1], step, jnp.zeros_like(field))]
    ppermute x6 -> x0, starting transfers between devices: 14 us -> none  [the longest x3 8.91 us: padded_2(): before = lax.ppermute(last, axis, up)]
    ppermute x6 -> x0, waiting for transfers between devices: 12 us -> none  [the longest x3 11 us: padded_2(): after = lax.ppermute(leading, axis, down)]
    slice x7 -> x0, local copies, waits for them, and re-layouts: 4.54 us -> none  [the longest x4 2.43 us: cell_tensor(): eta, lift, eps_one, eps_two = (params[0], params[1], params[2], params[3])]
  transfers between devices with their start and end apart: 8 -> 0, of which waited for: 7 -> 0; matrix products, arithmetic and copies ran while one was open for 2% -> 0% of each run, Pallas kernels for 0% -> 0%
where the time goes in v1:
time: 33.3 us; the launch traced here: 33 us
  Pallas kernels  28.2 us (85%)
  local copies, waits for them, and re-layouts  4.14 us (12%)
  between operations  0.66 us (2%)
    pallas_call x1, Pallas kernels, on_device(): pl.pallas_call(functools.partial(kernel, nx, nz, rows, cols, local), out_...  28.2 us
    unnamed x11, local copies, waits for them, and re-layouts  4.14 us

profile of v1, /device:TPU:1, one launch (start us, length us, event | category | flops | bytes accessed | tf_op | source)
XLA Modules:
  0.0 33.0 jit_solution(8834526481780482787)
XLA Ops:
  0.6 0.0 copy-start.3
  0.6 0.0 copy-start.2
  0.7 0.8 %copy.7.eps = f32[4,2]{1,0:T(4,128)S(1)} copy(f32[4,2]{0,1:T(2,128)} %param.9) | data formatting | bytes 64 | tf_op args[4]
  1.4 0.0 copy-done.3
  1.4 0.0 copy-done.2
  1.4 0.0 copy-start
  1.4 1.0 %copy-done = f32[6,4,16,256]{3,2,1,0:T(8,128)S(1)} copy-done((f32[6,4,16,256]{3,2,1,0:T(8,128)S(1)}, f32[6,4,16,256]{3,2,1,0:T(8,128)}, u32[]{:S(2)}) %copy-start) | copy-done | bytes 393240
  2.4 0.0 copy-start.1
  2.4 0.9 %copy-done.1 = f32[128,512]{1,0:T(8,128)S(1)} copy-done((f32[128,512]{1,0:T(8,128)S(1)}, f32[128,512]{1,0:T(8,128)}, u32[]{:S(2)}) %copy-start.1) | copy-done | bytes 262168
  3.4 28.2 %shard_map.68 = (f32[128,512]{1,0:T(8,128)S(1)}, f32[128,512]{1,0:T(8,128)S(1)}) custom-call(s32[4]{0:T(128)S(1)} %copy-done.2, s32[4]{0:T(128)S(1)} %copy-done.3, f32[4,2]{1,0:T(4,128)S(1)} %copy.7.eps, f32[128,512]{1,0:T(8,128)S(1)} %copy-done.1, f32[6,4,16,256]{3,2,1,0:T(8,128)S(1)} %copy-done), custom_call_target="tpu_custom_call" | custom-call | tf_op jit(solution)/shard_map/pallas_call | solution.py:297
  31.6 0.7 %copy.10 = f32[128,512]{1,0:T(8,128)} copy(f32[128,512]{1,0:T(8,128)S(1)} %get-tuple-element.4) | data formatting | bytes 524288
  32.3 0.7 %copy.11 = f32[128,512]{1,0:T(8,128)} copy(f32[128,512]{1,0:T(8,128)S(1)} %get-tuple-element.5) | data formatting | bytes 524288
Async XLA Ops:
  0.6 0.8 %copy-start.3 = (s32[4]{0:T(128)S(1)}, s32[4]{0:T(128)}, u32[]{:S(2)}) copy-start(s32[4]{0:T(128)} %block.1) | copy-start | bytes 52
  0.6 0.8 %copy-start.2 = (s32[4]{0:T(128)S(1)}, s32[4]{0:T(128)}, u32[]{:S(2)}) copy-start(s32[4]{0:T(128)} %slope.1) | copy-start | bytes 52
  1.4 1.0 %copy-start = (f32[6,4,16,256]{3,2,1,0:T(8,128)S(1)}, f32[6,4,16,256]{3,2,1,0:T(8,128)}, u32[]{:S(2)}) copy-start(f32[6,4,16,256]{3,2,1,0:T(8,128)} %cot.1) | copy-start | bytes 1179652
  2.4 0.9 %copy-start.1 = (f32[128,512]{1,0:T(8,128)S(1)}, f32[128,512]{1,0:T(8,128)}, u32[]{:S(2)}) copy-start(f32[128,512]{1,0:T(8,128)} %density.1) | copy-start | bytes 786436

commit v2 on v1

v2 whole, which is shorter than its diff:
```python
import functools
import math

import jax
import jax.numpy as jnp
from jax import lax
from jax.experimental import pallas as pl
from jax.experimental.pallas import tpu as pltpu
from jax.sharding import PartitionSpec as P

SUB = 8
RADIUS = 32
SLOPES = 5
LANES = 128
BAND_COLS = 256
STEEP = 32.0
MESH = pl.DeviceIdType.MESH
F32 = jnp.float32
BF16 = jnp.bfloat16
NEAR = [(dx, dz) for dx in (-1, 0, 1) for dz in (-1, 0, 1) if (dx, dz) != (0, 0)]


def split(value, terms):
    parts = []
    for _ in range(terms):
        part = value.astype(BF16)
        parts.append(part)
        value = value - part.astype(F32)
    return parts


def iota(shape, dim):
    return lax.broadcasted_iota(jnp.int32, shape, dim)


def taps(offset):
    return jnp.maximum(RADIUS + 1 - jnp.abs(offset), 0).astype(F32).astype(BF16)


def col_band():
    shape = (BAND_COLS + 2 * LANES, BAND_COLS)
    return taps(iota(shape, 0) - LANES - iota(shape, 1))


def row_band(height):
    shape = (height, height + 2 * RADIUS)
    return taps(iota(shape, 1) - RADIUS - iota(shape, 0))


def pool_values(cell, place, other):
    offset = (2 * (place % SUB) + 1 - SUB).astype(F32) / 2.0
    inside = place // SUB == cell % other
    values = jnp.where(cell < other, 1.0, offset) / float(SUB)
    return jnp.where(inside, values, 0.0).astype(BF16)


def col_pool(width):
    shape = (width, 2 * width // SUB)
    return pool_values(iota(shape, 1), iota(shape, 0), width // SUB)


def col_pool_t(width):
    shape = (2 * width // SUB, width)
    return pool_values(iota(shape, 0), iota(shape, 1), width // SUB)


def row_pool(height):
    shape = (2 * height // SUB, height)
    return pool_values(iota(shape, 0), iota(shape, 1), height // SUB)


def row_pool_t(height):
    shape = (height, 2 * height // SUB)
    return pool_values(iota(shape, 1), iota(shape, 0), height // SUB)


def dot(a, b):
    return jnp.dot(a, b, preferred_element_type=F32)


def smooth(pad, band_c, band_r, height, width, terms):
    scale = 1.0 / float((RADIUS + 1) ** 4)
    out = []
    for start in range(0, width, BAND_COLS):
        part = pad[:, start : start + BAND_COLS + 2 * LANES]
        across = sum(dot(x, band_c[...]) for x in split(part, terms))
        total = sum(dot(band_r[...], x) for x in split(across, terms))
        out.append(total * scale)
    return out


def pack_cols(block):
    groups = LANES // RADIUS
    height = block.shape[0] // groups
    lane = iota((1, LANES), 1)
    out = block[:height]
    for j in range(1, groups):
        moved = pltpu.roll(block[j * height : (j + 1) * height], j * RADIUS, 1)
        out = jnp.where(lane >= j * RADIUS, moved, out)
    return out


def kernel(nx, nz, rows, cols, local, slope, block, eps_hbm, density_hbm, cot_hbm, grad_out, dens_out,
           pad, gpad, strip_out, strip_in, cot, eps, stage, recv, power, soft, result,
           band_c, band_r, pool_c, back_c, pool_r2, back_r2,
           in_sem, out_sem, halo_send, halo_recv, cot_send, cot_recv):
    x = lax.axis_index("xy")
    z = lax.axis_index("gz")
    cells_x, cells_y = rows // SUB, cols // SUB
    tall, wide = rows + 2 * RADIUS, cols + 2 * LANES
    mid_r, mid_c = pl.ds(RADIUS, rows), pl.ds(LANES, cols)
    groups = LANES // RADIUS

    fetch_density = pltpu.make_async_copy(density_hbm, pad.at[mid_r, mid_c], in_sem.at[0])
    fetch_cot = pltpu.make_async_copy(cot_hbm, cot, in_sem.at[1])
    fetch_eps = pltpu.make_async_copy(eps_hbm, eps, in_sem.at[2])
    fetch_density.start()
    fetch_eps.start()
    fetch_cot.start()

    def exists(dx, dz):
        ok = None
        for pos, delta, count in ((x, dx, nx), (z, dz, nz)):
            if delta == -1:
                here = pos > 0
            elif delta == 1:
                here = pos < count - 1
            else:
                continue
            ok = here if ok is None else jnp.logical_and(ok, here)
        return ok

    for ref in (pad, gpad):
        ref[0:RADIUS, mid_c] = jnp.zeros((RADIUS, cols), F32)
        ref[RADIUS + rows : tall, mid_c] = jnp.zeros((RADIUS, cols), F32)
    strip_in[...] = jnp.zeros(strip_in.shape, F32)

    barrier = pltpu.get_barrier_semaphore()
    far = [(dx, dz) for dx, dz in NEAR if dx != 0]
    for k in range(1, nz):
        pl.semaphore_signal(barrier, inc=1, device_id=(x, lax.rem(z + k, nz)), device_id_type=MESH)
    for dx, dz in far:
        @pl.when(exists(dx, dz))
        def _():
            pl.semaphore_signal(barrier, inc=1, device_id=(x + dx, z + dz), device_id_type=MESH)

    quarter, corner = rows // groups, RADIUS // groups
    spots = {0: (0, quarter), -1: (quarter, corner), 1: (quarter + corner, corner)}

    def pack_strips(source, phase):
        for side, start in ((0, 0), (1, cols - LANES)):
            edge = source[RADIUS : RADIUS + rows, LANES + start : 2 * LANES + start]
            if side == 1:
                edge = pltpu.roll(edge, RADIUS, 1)
            strip_out[phase, side, 0:quarter] = pack_cols(edge)
            strip_out[phase, side, quarter : quarter + corner] = pack_cols(edge[:RADIUS])
            strip_out[phase, side, quarter + corner :] = pack_cols(edge[rows - RADIUS :])

    def unpack_strips(target, phase):
        for side, column, shift in ((0, 0, LANES - RADIUS), (1, LANES + cols, 0)):
            for first, height, at in ((0, quarter, RADIUS), (quarter, corner, RADIUS + rows), (quarter + corner, corner, 0)):
                packed = strip_in[phase, side, first : first + height]
                for j in range(groups):
                    turn = (shift - j * RADIUS) % LANES
                    moved = pltpu.roll(packed, turn, 1) if turn else packed
                    target[at + j * height : at + (j + 1) * height, column : column + LANES] = moved

    def halo(target, phase, d):
        dx, dz = NEAR[d]
        if dz == 0:
            src = target.at[pl.ds(RADIUS if dx < 0 else rows, RADIUS), mid_c]
            dst = target.at[pl.ds(RADIUS + rows if dx < 0 else 0, RADIUS), mid_c]
        else:
            at = pl.ds(*spots[dx])
            src = strip_out.at[phase, 0 if dz < 0 else 1, at]
            dst = strip_in.at[phase, 1 if dz < 0 else 0, at]
        return pltpu.make_async_remote_copy(
            src_ref=src, dst_ref=dst, send_sem=halo_send.at[phase, d], recv_sem=halo_recv.at[phase, d],
            device_id=(x + dx, z + dz), device_id_type=MESH)

    def halo_each(target, phase, what, flat=(True, False)):
        for d, (dx, dz) in enumerate(NEAR):
            if (dz == 0) in flat:
                copy = halo(target, phase, d)
                where = exists(-dx, -dz) if what == "wait_recv" else exists(dx, dz)
                pl.when(where)(getattr(copy, what))

    fetch_density.wait()
    pack_strips(pad, 0)
    band_c[...] = col_band()
    band_r[...] = row_band(rows)
    pl.semaphore_wait(barrier, nz - 1 + sum(jnp.where(exists(dx, dz), 1, 0) for dx, dz in far))
    halo_each(pad, 0, "start")

    half = iota((1, LANES), 1) < cells_y
    swap = lambda v: pltpu.roll(v, cells_y, 1)
    comps = cot.shape[0]
    fetch_eps.wait()
    lines = []
    for k in range(local // 2):
        a, b = 2 * k, 2 * k + 1
        lines.append(jnp.where(half, slope[a].astype(F32), slope[b].astype(F32)))
        pair = jnp.where(half, block[a], block[b])
        for j in range(2):
            line = jnp.zeros((1, LANES), F32)
            for m in range(eps.shape[1]):
                line = jnp.where(pair == m, eps[j : j + 1, m : m + 1], line)
            lines.append(line)
    lines.append(jnp.zeros((cells_x - len(lines), LANES), F32))
    lines = jnp.concatenate(lines, axis=0)
    fetch_cot.wait()
    for c in range(comps):
        for k in range(local // 2):
            for h in range(nz // 2):
                a = cot[c, 2 * k, :, h * LANES : (h + 1) * LANES]
                b = cot[c, 2 * k + 1, :, h * LANES : (h + 1) * LANES]
                stage[2 * h, c * (local // 2) + k] = jnp.where(half, a, swap(b))
                stage[2 * h + 1, c * (local // 2) + k] = jnp.where(half, swap(a), b)
    for g in range(nz):
        stage[g, comps * (local // 2)] = lines

    def cot_copy(k, outgoing):
        peer = lax.rem(z + k, nz)
        slot = z if outgoing else peer
        return pltpu.make_async_remote_copy(
            src_ref=stage.at[peer], dst_ref=recv.at[slot], send_sem=cot_send.at[k], recv_sem=cot_recv.at[slot],
            device_id=(x, peer), device_id_type=MESH)

    for k in range(1, nz):
        cot_copy(k, True).start()

    pool_c[...] = col_pool(cols)
    back_c[...] = col_pool_t(cols)
    pool_r = row_pool(rows)
    pool_r2[...] = jnp.concatenate([pool_r, pool_r], axis=1)
    back_r = row_pool_t(rows)
    back_r2[...] = jnp.concatenate([back_r, back_r], axis=1)

    halo_each(pad, 0, "wait_recv")
    unpack_strips(pad, 0)
    for i, part in enumerate(smooth(pad, band_c, band_r, rows, cols, 3)):
        power[:, i * BAND_COLS : (i + 1) * BAND_COLS] = jnp.exp(STEEP * (0.5 - part))

    moments = []
    for c in range(SLOPES):
        fill = 1.0 / (1.0 + power[...] * math.exp(STEEP * 0.02 * (c - 2)))
        soft[c] = fill * (1.0 - fill)
        upper, lower = split(fill, 2)
        pooled = dot(upper, pool_c[...]) + dot(lower, pool_c[...])
        cell = dot(pool_r2[...], jnp.concatenate(split(pooled, 2), axis=0))
        top, low = cell[:cells_x], cell[cells_x:]
        turned = swap(top)
        moments.append((jnp.where(half, top, turned), jnp.where(half, low, swap(low)), jnp.where(half, turned, top)))

    totals = [[jnp.zeros((cells_x, LANES), F32)] * 3 for _ in range(SLOPES)]
    for g in range(nz):
        slot = lax.rem(z + g, nz)
        if g:
            cot_copy(g, False).wait_recv()
        held = recv if g else stage
        for k in range(local // 2):
            at = comps * (local // 2)
            kind, e1, e2 = (held[slot, at, 3 * k + j : 3 * k + j + 1, :] for j in range(3))
            cxx, cyy, czz, cxy, cxz, cyz = (held[slot, c * (local // 2) + k] for c in range(comps))
            masks = [jnp.broadcast_to(kind == float(c), (cells_x, LANES)) for c in range(SLOPES)]
            frac, gx, gy = moments[0]
            for c in range(1, SLOPES):
                frac, gx, gy = (jnp.where(masks[c], new, old) for new, old in zip(moments[c], (frac, gx, gy)))
            cz = 0.2 * (1.0 + kind)
            step = e1 - e2
            inv2 = 1.0 / e2
            inv_step = 1.0 / e1 - inv2
            norm = 1.0 / (gx * gx + gy * gy + cz * cz)
            mean = e2 + frac * step
            harm = 1.0 / (inv2 + frac * inv_step)
            weight = (harm - mean) * norm
            px = cxx * gx + cxy * gy + cxz * cz
            py = cyy * gy + cyz * cz
            quad = (gx * px + gy * py + cz * cz * czz) * norm
            adjoint = ((cxx + cyy + czz - quad) * step - quad * harm * harm * inv_step,
                       weight * (px + (cxx - 2.0 * quad) * gx),
                       weight * (py + (cyy - 2.0 * quad) * gy + cxy * gx))
            for c in range(SLOPES):
                totals[c] = [old + jnp.where(masks[c], new, 0.0) for old, new in zip(totals[c], adjoint)]

    zs = []
    for d_frac, d_gx, d_gy in totals:
        d_frac, d_gx, d_gy = (v + swap(v) for v in (d_frac, d_gx, d_gy))
        zs += [jnp.where(half, d_frac, d_gy), jnp.where(half, d_gx, 0.0)]
    upper, lower = split(jnp.concatenate(zs, axis=0) * STEEP, 2)
    spread = dot(upper, back_c[...]) + dot(lower, back_c[...])
    deep = 2 * cells_x
    own = None
    for c in range(SLOPES):
        pixels = dot(back_r2[...], jnp.concatenate(split(spread[c * deep : (c + 1) * deep], 2), axis=0))
        own = pixels * soft[c] if c == 0 else own + pixels * soft[c]

    gpad[mid_r, mid_c] = own
    halo_each(gpad, 1, "start", (True,))
    pack_strips(gpad, 1)
    halo_each(gpad, 1, "start", (False,))
    write_grad = pltpu.make_async_copy(gpad.at[mid_r, mid_c], grad_out, out_sem.at[0])
    write_grad.start()
    halo_each(gpad, 1, "wait_recv")
    unpack_strips(gpad, 1)
    writes = [write_grad]
    for i, part in enumerate(smooth(gpad, band_c, band_r, rows, cols, 2)):
        at = pl.ds(i * BAND_COLS, BAND_COLS)
        result[:, at] = part
        write = pltpu.make_async_copy(result.at[:, at], dens_out.at[:, at], out_sem.at[i + 1])
        write.start()
        writes.append(write)

    halo_each(pad, 0, "wait_send")
    halo_each(gpad, 1, "wait_send")
    for k in range(1, nz):
        cot_copy(k, True).wait_send()
    for write in writes:
        write.wait()


def on_device(density, cot, slope, layer_block, block_eps, nx, nz):
    rows, cols = density.shape
    comps, local = cot.shape[:2]
    cells_x = rows // SUB
    tall, wide = rows + 2 * RADIUS, cols + 2 * LANES
    packed = (nz, comps * (local // 2) + 1, cells_x, LANES)
    strips = (2, 2, (rows + 2 * RADIUS) * RADIUS // LANES, LANES)
    hbm = pl.BlockSpec(memory_space=pltpu.HBM)
    smem = pl.BlockSpec(memory_space=pltpu.SMEM)
    dma = pltpu.SemaphoreType.DMA
    near = len(NEAR)
    shape = jax.ShapeDtypeStruct((rows, cols), F32)
    return pl.pallas_call(
        functools.partial(kernel, nx, nz, rows, cols, local),
        out_shape=(shape, shape),
        in_specs=[smem, smem, hbm, hbm, hbm],
        out_specs=(hbm, hbm),
        scratch_shapes=[
            pltpu.VMEM((tall, wide), F32),
            pltpu.VMEM((tall, wide), F32),
            pltpu.VMEM(strips, F32),
            pltpu.VMEM(strips, F32),
            pltpu.VMEM(cot.shape, F32),
            pltpu.VMEM(block_eps.shape[::-1], F32),
            pltpu.VMEM(packed, F32),
            pltpu.VMEM(packed, F32),
            pltpu.VMEM((rows, cols), F32),
            pltpu.VMEM((SLOPES, rows, cols), F32),
            pltpu.VMEM((rows, cols), F32),
            pltpu.VMEM((BAND_COLS + 2 * LANES, BAND_COLS), BF16),
            pltpu.VMEM((rows, tall), BF16),
            pltpu.VMEM((cols, LANES), BF16),
            pltpu.VMEM((LANES, cols), BF16),
            pltpu.VMEM((2 * cells_x, 2 * rows), BF16),
            pltpu.VMEM((rows, 4 * cells_x), BF16),
            dma((3,)), dma((1 + cols // BAND_COLS,)),
            dma((2, near)), dma((2, near)), dma((nz,)), dma((nz,)),
        ],
        compiler_params=pltpu.CompilerParams(
            collective_id=0, has_side_effects=True, vmem_limit_bytes=60 * 1024 * 1024),
    )(slope, layer_block, block_eps.T, density, cot)


def solution(mesh):
    body = functools.partial(on_device, nx=mesh.shape["xy"], nz=mesh.shape["gz"])
    return jax.shard_map(
        body,
        mesh=mesh,
        in_specs=(P("xy", "gz"), P(None, "gz", "xy", None), P("gz"), P("gz"), P()),
        out_specs=(P("xy", "gz"), P("xy", "gz")),
        check_vma=False,
    )
```

time: 33.3 us -> 25.8 us (0.77)
  Pallas kernels: 28.2 us -> 22.6 us
  local copies, waits for them, and re-layouts: 4.14 us -> 2.42 us
    pallas_call x1, Pallas kernels: 28.2 us -> 22.6 us  [on_device(): pl.pallas_call(functools.partial(kernel, nx, nz, rows, cols, local), out_...]
    unnamed x11 -> x4, local copies, waits for them, and re-layouts: 4.14 us -> 2.42 us
where the time goes in v2:
time: 25.8 us; the launch traced here: 25.7 us
  Pallas kernels  22.6 us (88%)
  local copies, waits for them, and re-layouts  2.42 us (9%)
  between operations  0.65 us (3%)
    pallas_call x1, Pallas kernels, on_device(): pl.pallas_call(functools.partial(kernel, nx, nz, rows, cols, local), out_...  22.6 us
    unnamed x4, local copies, waits for them, and re-layouts  2.42 us

profile of v2, /device:TPU:1, one launch (start us, length us, event | category | flops | bytes accessed | tf_op | source)
XLA Modules:
  0.0 25.7 jit_solution(14183680011992262879)
XLA Ops:
  0.6 22.6 %shard_map.68 = (f32[128,512]{1,0:T(8,128)}, f32[128,512]{1,0:T(8,128)}) custom-call(s32[4]{0:T(128)} %slope.1, s32[4]{0:T(128)} %block.1, f32[2,4]{1,0:T(2,128)} %bitcast.1, f32[128,512]{1,0:T(8,128)} %density_hbm.1, f32[6,4,16,256]{3,2,1,0:T(8,128)} %cot_hbm.1), custom_call_target="tpu_custom_call" | custom-call | tf_op jit(solution)/shard_map/pallas_call | solution.py:334
  23.2 0.0 copy-start
  23.2 1.7 %copy.9 = f32[128,512]{1,0:T(8,128)} copy(f32[128,512]{1,0:T(8,128)} %get-tuple-element.4) | data formatting | bytes 524288
  25.0 0.0 copy-done
  25.0 0.7 %copy.10 = f32[128,512]{1,0:T(8,128)} copy(f32[128,512]{1,0:T(8,128)S(1)} %copy-done) | data formatting | bytes 524288
Async XLA Ops:
  23.2 1.7 %copy-start = (f32[128,512]{1,0:T(8,128)S(1)}, f32[128,512]{1,0:T(8,128)}, u32[]{:S(2)}) copy-start(f32[128,512]{1,0:T(8,128)} %get-tuple-element.5) | copy-start | bytes 786436

commit v3 on v2

--- a/solution.py
+++ b/solution.py
@@ -100,8 +100,43 @@
     return out
 
 
-def kernel(nx, nz, rows, cols, local, slope, block, eps_hbm, density_hbm, cot_hbm, grad_out, dens_out,
-           pad, gpad, strip_out, strip_in, cot, eps, stage, recv, power, soft, result,
+def unpack_strips(strips, target, rows, cols):
+    groups = LANES // RADIUS
+    quarter, corner = rows // groups, RADIUS // groups
+    for side, column, shift in ((0, 0, LANES - RADIUS), (1, LANES + cols, 0)):
+        for first, height, at in ((0, quarter, RADIUS), (quarter, corner, RADIUS + rows), (quarter + corner, corner, 0)):
+            packed = strips[side, first : first + height]
+            for j in range(groups):
+                turn = (shift - j * RADIUS) % LANES
+                moved = pltpu.roll(packed, turn, 1) if turn else packed
+                target[at + j * height : at + (j + 1) * height, column : column + LANES] = moved
+
+
+def finish(rows, cols, flat_hbm, strips_hbm, grad_out, dens_out, pad, strips, result, band_c, band_r, in_sem, out_sem):
+    mid_c = pl.ds(LANES, cols)
+    fetch_flat = pltpu.make_async_copy(flat_hbm, pad.at[:, mid_c], in_sem.at[0])
+    fetch_strips = pltpu.make_async_copy(strips_hbm, strips, in_sem.at[1])
+    fetch_flat.start()
+    fetch_strips.start()
+    band_c[...] = col_band()
+    band_r[...] = row_band(rows)
+    fetch_strips.wait()
+    unpack_strips(strips, pad, rows, cols)
+    fetch_flat.wait()
+    writes = [pltpu.make_async_copy(pad.at[pl.ds(RADIUS, rows), mid_c], grad_out, out_sem.at[0])]
+    writes[0].start()
+    for i, part in enumerate(smooth(pad, band_c, band_r, rows, cols, 2)):
+        at = pl.ds(i * BAND_COLS, BAND_COLS)
+        result[:, at] = part
+        write = pltpu.make_async_copy(result.at[:, at], dens_out.at[:, at], out_sem.at[i + 1])
+        write.start()
+        writes.append(write)
+    for write in writes:
+        write.wait()
+
+
+def kernel(nx, nz, rows, cols, local, slope, block, eps_hbm, density_hbm, cot_hbm, flat_out, strips_out,
+           pad, gpad, strip_out, strip_in, cot, eps, stage, recv, power, soft,
            band_c, band_r, pool_c, back_c, pool_r2, back_r2,
            in_sem, out_sem, halo_send, halo_recv, cot_send, cot_recv):
     x = lax.axis_index("xy")
@@ -155,15 +190,6 @@
             strip_out[phase, side, 0:quarter] = pack_cols(edge)
             strip_out[phase, side, quarter : quarter + corner] = pack_cols(edge[:RADIUS])
             strip_out[phase, side, quarter + corner :] = pack_cols(edge[rows - RADIUS :])
-
-    def unpack_strips(target, phase):
-        for side, column, shift in ((0, 0, LANES - RADIUS), (1, LANES + cols, 0)):
-            for first, height, at in ((0, quarter, RADIUS), (quarter, corner, RADIUS + rows), (quarter + corner, corner, 0)):
-                packed = strip_in[phase, side, first : first + height]
-                for j in range(groups):
-                    turn = (shift - j * RADIUS) % LANES
-                    moved = pltpu.roll(packed, turn, 1) if turn else packed
-                    target[at + j * height : at + (j + 1) * height, column : column + LANES] = moved
 
     def halo(target, phase, d):
         dx, dz = NEAR[d]
@@ -187,11 +213,6 @@
 
     fetch_density.wait()
     pack_strips(pad, 0)
-    band_c[...] = col_band()
-    band_r[...] = row_band(rows)
-    pl.semaphore_wait(barrier, nz - 1 + sum(jnp.where(exists(dx, dz), 1, 0) for dx, dz in far))
-    halo_each(pad, 0, "start")
-
     half = iota((1, LANES), 1) < cells_y
     swap = lambda v: pltpu.roll(v, cells_y, 1)
     comps = cot.shape[0]
@@ -206,7 +227,7 @@
             for m in range(eps.shape[1]):
                 line = jnp.where(pair == m, eps[j : j + 1, m : m + 1], line)
             lines.append(line)
-    lines.append(jnp.zeros((cells_x - len(lines), LANES), F32))
+    lines.append(jnp.zeros((8 - len(lines), LANES), F32))
     lines = jnp.concatenate(lines, axis=0)
     fetch_cot.wait()
     for c in range(comps):
@@ -214,10 +235,10 @@
             for h in range(nz // 2):
                 a = cot[c, 2 * k, :, h * LANES : (h + 1) * LANES]
                 b = cot[c, 2 * k + 1, :, h * LANES : (h + 1) * LANES]
-                stage[2 * h, c * (local // 2) + k] = jnp.where(half, a, swap(b))
-                stage[2 * h + 1, c * (local // 2) + k] = jnp.where(half, swap(a), b)
+                stage[2 * h, pl.ds((c * (local // 2) + k) * cells_x, cells_x)] = jnp.where(half, a, swap(b))
+                stage[2 * h + 1, pl.ds((c * (local // 2) + k) * cells_x, cells_x)] = jnp.where(half, swap(a), b)
     for g in range(nz):
-        stage[g, comps * (local // 2)] = lines
+        stage[g, pl.ds(comps * (local // 2) * cells_x, 8)] = lines
 
     def cot_copy(k, outgoing):
         peer = lax.rem(z + k, nz)
@@ -226,9 +247,14 @@
             src_ref=stage.at[peer], dst_ref=recv.at[slot], send_sem=cot_send.at[k], recv_sem=cot_recv.at[slot],
             device_id=(x, peer), device_id_type=MESH)
 
+    pl.semaphore_wait(barrier, nz - 1 + sum(jnp.where(exists(dx, dz), 1, 0) for dx, dz in far))
+    halo_each(pad, 0, "start")
+
     for k in range(1, nz):
         cot_copy(k, True).start()
 
+    band_c[...] = col_band()
+    band_r[...] = row_band(rows)
     pool_c[...] = col_pool(cols)
     back_c[...] = col_pool_t(cols)
     pool_r = row_pool(rows)
@@ -237,7 +263,7 @@
     back_r2[...] = jnp.concatenate([back_r, back_r], axis=1)
 
     halo_each(pad, 0, "wait_recv")
-    unpack_strips(pad, 0)
+    unpack_strips(strip_in.at[0], pad, rows, cols)
     for i, part in enumerate(smooth(pad, band_c, band_r, rows, cols, 3)):
         power[:, i * BAND_COLS : (i + 1) * BAND_COLS] = jnp.exp(STEEP * (0.5 - part))
 
@@ -259,9 +285,9 @@
             cot_copy(g, False).wait_recv()
         held = recv if g else stage
         for k in range(local // 2):
-            at = comps * (local // 2)
-            kind, e1, e2 = (held[slot, at, 3 * k + j : 3 * k + j + 1, :] for j in range(3))
-            cxx, cyy, czz, cxy, cxz, cyz = (held[slot, c * (local // 2) + k] for c in range(comps))
+            at = comps * (local // 2) * cells_x + 3 * k
+            kind, e1, e2 = (held[slot, at + j : at + j + 1, :] for j in range(3))
+            cxx, cyy, czz, cxy, cxz, cyz = (held[slot, pl.ds((c * (local // 2) + k) * cells_x, cells_x)] for c in range(comps))
             masks = [jnp.broadcast_to(kind == float(c), (cells_x, LANES)) for c in range(SLOPES)]
             frac, gx, gy = moments[0]
             for c in range(1, SLOPES):
@@ -299,17 +325,15 @@
     halo_each(gpad, 1, "start", (True,))
     pack_strips(gpad, 1)
     halo_each(gpad, 1, "start", (False,))
-    write_grad = pltpu.make_async_copy(gpad.at[mid_r, mid_c], grad_out, out_sem.at[0])
-    write_grad.start()
+    writes = [pltpu.make_async_copy(gpad.at[mid_r, mid_c], flat_out.at[mid_r], out_sem.at[0])]
+    writes[0].start()
     halo_each(gpad, 1, "wait_recv")
-    unpack_strips(gpad, 1)
-    writes = [write_grad]
-    for i, part in enumerate(smooth(gpad, band_c, band_r, rows, cols, 2)):
-        at = pl.ds(i * BAND_COLS, BAND_COLS)
-        result[:, at] = part
-        write = pltpu.make_async_copy(result.at[:, at], dens_out.at[:, at], out_sem.at[i + 1])
+    top, bottom = pl.ds(0, RADIUS), pl.ds(RADIUS + rows, RADIUS)
+    writes += [pltpu.make_async_copy(gpad.at[top, mid_c], flat_out.at[top], out_sem.at[1]),
+               pltpu.make_async_copy(gpad.at[bottom, mid_c], flat_out.at[bottom], out_sem.at[2]),
+               pltpu.make_async_copy(strip_in.at[1], strips_out, out_sem.at[3])]
+    for write in writes[1:]:
         write.start()
-        writes.append(write)
 
     halo_each(pad, 0, "wait_send")
     halo_each(gpad, 1, "wait_send")
@@ -324,16 +348,16 @@
     comps, local = cot.shape[:2]
     cells_x = rows // SUB
     tall, wide = rows + 2 * RADIUS, cols + 2 * LANES
-    packed = (nz, comps * (local // 2) + 1, cells_x, LANES)
+    packed = (nz, comps * (local // 2) * cells_x + 8, LANES)
     strips = (2, 2, (rows + 2 * RADIUS) * RADIUS // LANES, LANES)
     hbm = pl.BlockSpec(memory_space=pltpu.HBM)
     smem = pl.BlockSpec(memory_space=pltpu.SMEM)
     dma = pltpu.SemaphoreType.DMA
     near = len(NEAR)
     shape = jax.ShapeDtypeStruct((rows, cols), F32)
-    return pl.pallas_call(
+    flat, packed_strips = pl.pallas_call(
         functools.partial(kernel, nx, nz, rows, cols, local),
-        out_shape=(shape, shape),
+        out_shape=(jax.ShapeDtypeStruct((tall, cols), F32), jax.ShapeDtypeStruct(strips[1:], F32)),
         in_specs=[smem, smem, hbm, hbm, hbm],
         out_specs=(hbm, hbm),
         scratch_shapes=[
@@ -347,19 +371,33 @@
             pltpu.VMEM(packed, F32),
             pltpu.VMEM((rows, cols), F32),
             pltpu.VMEM((SLOPES, rows, cols), F32),
-            pltpu.VMEM((rows, cols), F32),
             pltpu.VMEM((BAND_COLS + 2 * LANES, BAND_COLS), BF16),
             pltpu.VMEM((rows, tall), BF16),
             pltpu.VMEM((cols, LANES), BF16),
             pltpu.VMEM((LANES, cols), BF16),
             pltpu.VMEM((2 * cells_x, 2 * rows), BF16),
             pltpu.VMEM((rows, 4 * cells_x), BF16),
-            dma((3,)), dma((1 + cols // BAND_COLS,)),
+            dma((3,)), dma((4,)),
             dma((2, near)), dma((2, near)), dma((nz,)), dma((nz,)),
         ],
         compiler_params=pltpu.CompilerParams(
             collective_id=0, has_side_effects=True, vmem_limit_bytes=60 * 1024 * 1024),
     )(slope, layer_block, block_eps.T, density, cot)
+    return pl.pallas_call(
+        functools.partial(finish, rows, cols),
+        out_shape=(shape, shape),
+        in_specs=[hbm, hbm],
+        out_specs=(hbm, hbm),
+        scratch_shapes=[
+            pltpu.VMEM((tall, wide), F32),
+            pltpu.VMEM(strips[1:], F32),
+            pltpu.VMEM((rows, cols), F32),
+            pltpu.VMEM((BAND_COLS + 2 * LANES, BAND_COLS), BF16),
+            pltpu.VMEM((rows, tall), BF16),
+            dma((2,)), dma((1 + cols // BAND_COLS,)),
+        ],
+        compiler_params=pltpu.CompilerParams(vmem_limit_bytes=60 * 1024 * 1024),
+    )(flat, packed_strips)
 
 
 def solution(mesh):

time: 25.8 us -> 24.8 us (0.961)
  local copies, waits for them, and re-layouts: 2.42 us -> 0 us
  Pallas kernels: 22.6 us -> 24 us
    pallas_call x0 -> x1, Pallas kernels: none -> 2.64 us  [on_device(): pl.pallas_call(functools.partial(finish, rows, cols), out_shape=(shape, s...]
    unnamed x4 -> x0, local copies, waits for them, and re-layouts: 2.42 us -> none
    pallas_call x1, Pallas kernels: 22.6 us -> 21.4 us  [on_device(): pl.pallas_call(functools.partial(kernel, nx, nz, rows, cols, local), out_...]
where the time goes in v3:
time: 24.8 us; the launch traced here: 24.6 us
  Pallas kernels  24 us (97%)
  between operations  0.64 us (3%)
    pallas_call x1, Pallas kernels, on_device(): pl.pallas_call(functools.partial(kernel, nx, nz, rows, cols, local), out_...  21.4 us
    pallas_call x1, Pallas kernels, on_device(): pl.pallas_call(functools.partial(finish, rows, cols), out_shape=(shape, s...  2.64 us

profile of v3, /device:TPU:1, one launch (start us, length us, event | category | flops | bytes accessed | tf_op | source)
XLA Modules:
  0.0 24.6 jit_solution(7908372437937165019)
XLA Ops:
  0.6 21.4 %shard_map.68 = (f32[192,512]{1,0:T(8,128)}, f32[2,48,128]{2,1,0:T(8,128)}) custom-call(s32[4]{0:T(128)} %slope.1, s32[4]{0:T(128)} %block.1, f32[2,4]{1,0:T(2,128)} %bitcast.1, f32[128,512]{1,0:T(8,128)} %density_hbm.1, f32[6,4,16,256]{3,2,1,0:T(8,128)} %cot_hbm.1), custom_call_target="tpu_custom_call" | custom-call | tf_op jit(solution)/shard_map/pallas_call | solution.py:358
  22.0 2.6 %shard_map.69 = (f32[128,512]{1,0:T(8,128)}, f32[128,512]{1,0:T(8,128)}) custom-call(f32[192,512]{1,0:T(8,128)} %get-tuple-element.4.flat_hbm, f32[2,48,128]{2,1,0:T(8,128)} %get-tuple-element.5.strips_hbm), custom_call_target="tpu_custom_call" | custom-call | tf_op jit(solution)/shard_map/pallas_call | solution.py:386

commit v4 on v3

--- a/solution.py
+++ b/solution.py
@@ -235,23 +235,26 @@
             for h in range(nz // 2):
                 a = cot[c, 2 * k, :, h * LANES : (h + 1) * LANES]
                 b = cot[c, 2 * k + 1, :, h * LANES : (h + 1) * LANES]
-                stage[2 * h, pl.ds((c * (local // 2) + k) * cells_x, cells_x)] = jnp.where(half, a, swap(b))
-                stage[2 * h + 1, pl.ds((c * (local // 2) + k) * cells_x, cells_x)] = jnp.where(half, swap(a), b)
+                stage[2 * h, pl.ds(8 + (k * comps + c) * cells_x, cells_x)] = jnp.where(half, a, swap(b))
+                stage[2 * h + 1, pl.ds(8 + (k * comps + c) * cells_x, cells_x)] = jnp.where(half, swap(a), b)
     for g in range(nz):
-        stage[g, pl.ds(comps * (local // 2) * cells_x, 8)] = lines
-
-    def cot_copy(k, outgoing):
+        stage[g, pl.ds(0, 8)] = lines
+
+    def cot_copy(part, k, outgoing):
+        at = pl.ds(8 + part * comps * cells_x if part else 0, comps * cells_x + (0 if part else 8))
         peer = lax.rem(z + k, nz)
         slot = z if outgoing else peer
         return pltpu.make_async_remote_copy(
-            src_ref=stage.at[peer], dst_ref=recv.at[slot], send_sem=cot_send.at[k], recv_sem=cot_recv.at[slot],
+            src_ref=stage.at[peer, at], dst_ref=recv.at[slot, at],
+            send_sem=cot_send.at[part, k], recv_sem=cot_recv.at[part, slot],
             device_id=(x, peer), device_id_type=MESH)
 
     pl.semaphore_wait(barrier, nz - 1 + sum(jnp.where(exists(dx, dz), 1, 0) for dx, dz in far))
     halo_each(pad, 0, "start")
 
-    for k in range(1, nz):
-        cot_copy(k, True).start()
+    for part in range(local // 2):
+        for k in range(1, nz):
+            cot_copy(part, k, True).start()
 
     band_c[...] = col_band()
     band_r[...] = row_band(rows)
@@ -279,15 +282,15 @@
         moments.append((jnp.where(half, top, turned), jnp.where(half, low, swap(low)), jnp.where(half, turned, top)))
 
     totals = [[jnp.zeros((cells_x, LANES), F32)] * 3 for _ in range(SLOPES)]
-    for g in range(nz):
-        slot = lax.rem(z + g, nz)
-        if g:
-            cot_copy(g, False).wait_recv()
-        held = recv if g else stage
-        for k in range(local // 2):
-            at = comps * (local // 2) * cells_x + 3 * k
+    for k in range(local // 2):
+        for g in range(nz):
+            slot = lax.rem(z + g, nz)
+            if g:
+                cot_copy(k, g, False).wait_recv()
+            held = recv if g else stage
+            at = 3 * k
             kind, e1, e2 = (held[slot, at + j : at + j + 1, :] for j in range(3))
-            cxx, cyy, czz, cxy, cxz, cyz = (held[slot, pl.ds((c * (local // 2) + k) * cells_x, cells_x)] for c in range(comps))
+            cxx, cyy, czz, cxy, cxz, cyz = (held[slot, pl.ds(8 + (k * comps + c) * cells_x, cells_x)] for c in range(comps))
             masks = [jnp.broadcast_to(kind == float(c), (cells_x, LANES)) for c in range(SLOPES)]
             frac, gx, gy = moments[0]
             for c in range(1, SLOPES):
@@ -338,7 +341,8 @@
     halo_each(pad, 0, "wait_send")
     halo_each(gpad, 1, "wait_send")
     for k in range(1, nz):
-        cot_copy(k, True).wait_send()
+        for part in range(local // 2):
+            cot_copy(part, k, True).wait_send()
     for write in writes:
         write.wait()
 
@@ -378,7 +382,7 @@
             pltpu.VMEM((2 * cells_x, 2 * rows), BF16),
             pltpu.VMEM((rows, 4 * cells_x), BF16),
             dma((3,)), dma((4,)),
-            dma((2, near)), dma((2, near)), dma((nz,)), dma((nz,)),
+            dma((2, near)), dma((2, near)), dma((local // 2, nz)), dma((local // 2, nz)),
         ],
         compiler_params=pltpu.CompilerParams(
             collective_id=0, has_side_effects=True, vmem_limit_bytes=60 * 1024 * 1024),

time: 24.8 us -> 24.8 us (level)
  no operation moved by 1% of the time
where the time goes in v4:
time: 24.8 us; the launch traced here: 24.6 us
  Pallas kernels  24 us (97%)
  between operations  0.64 us (3%)
    pallas_call x1, Pallas kernels, on_device(): pl.pallas_call(functools.partial(kernel, nx, nz, rows, cols, local), out_...  21.3 us
    pallas_call x1, Pallas kernels, on_device(): pl.pallas_call(functools.partial(finish, rows, cols), out_shape=(shape, s...  2.64 us

profile of v4, /device:TPU:1, one launch (start us, length us, event | category | flops | bytes accessed | tf_op | source)
XLA Modules:
  0.0 24.6 jit_solution(3411400306881695615)
XLA Ops:
  0.6 21.3 %shard_map.68 = (f32[192,512]{1,0:T(8,128)}, f32[2,48,128]{2,1,0:T(8,128)}) custom-call(s32[4]{0:T(128)} %slope.1, s32[4]{0:T(128)} %block.1, f32[2,4]{1,0:T(2,128)} %bitcast.1, f32[128,512]{1,0:T(8,128)} %density_hbm.1, f32[6,4,16,256]{3,2,1,0:T(8,128)} %cot_hbm.1), custom_call_target="tpu_custom_call" | custom-call | tf_op jit(solution)/shard_map/pallas_call | solution.py:362
  22.0 2.6 %shard_map.69 = (f32[128,512]{1,0:T(8,128)}, f32[128,512]{1,0:T(8,128)}) custom-call(f32[192,512]{1,0:T(8,128)} %get-tuple-element.4.flat_hbm, f32[2,48,128]{2,1,0:T(8,128)} %get-tuple-element.5.strips_hbm), custom_call_target="tpu_custom_call" | custom-call | tf_op jit(solution)/shard_map/pallas_call | solution.py:390
